TPU v7x, 32 devices: a whole 2x2x4 slice. The times are simulated.
32 devices in a mesh: dp: 8 (over z, y), ctx: 4 (over x, core).
Axes of the slice: x: 2, y: 2, z: 4, core: 2. Of those that a mesh axis runs over, the one named last changes fastest.
Arguments:
- queries: bfloat16 [8192, 512], P(('dp', 'ctx')), may hold values from -6 to 6
- key_rows: bfloat16 [8192, 512], P(('dp', 'ctx')), may hold values from -6 to 6
- value_rows: bfloat16 [8192, 512], P(('dp', 'ctx')), may hold values from -6 to 6
- grad_out: bfloat16 [8192, 512], P(('dp', 'ctx')), may hold values from -192 to 192
- rab_table: float32 [4, 13], replicated, may hold values from -1 to 1
- first_block: int32 [8, 4], P('dp'), may hold values from 0 to 3, as said below
- block_fill: int32 [8, 4], P('dp'), may hold values from 1 to 256, as said below
- block_order: int32 [8, 4], P('dp'), may hold values from 0 to 3, each once within a row
Outputs:
- grad_query: bfloat16 [8192, 512], P(('dp', 'ctx'))
- grad_key: bfloat16 [8192, 512], P(('dp', 'ctx'))
- grad_value: bfloat16 [8192, 512], P(('dp', 'ctx'))
- grad_rab: float32 [4, 13], replicated
Inputs may be any that keep to these rules, and one draw needn't show every extreme that they name: `block_order`: in each group every number appears once. `first_block`: each history covers consecutive logical blocks of its group, and an entry names the first of them. Logical block 0 starts a history that also covers block 1. Where a group has three or more blocks, its last logical block starts a history of its own. `block_fill`: valid events are the first ones of a block; every block but the last of its history has all 256.
All inputs are finite; a program needn't handle non-finite values.
Results may differ from a plain program's by a relative error of at most 0.0051.
Values may be sent and summed in bfloat16 or wider, within the bound.
A program may use at most 128 MiB of HBM per device.

v0:
```python
import jax
import jax.numpy as jnp
from jax import lax
from jax.sharding import PartitionSpec as P


def bucket_of(distance, bucket_total):
    value = distance + 1
    guess = jnp.floor(jnp.log2(value.astype(jnp.float32))).astype(jnp.int32)
    guess = jnp.clip(guess, 0, 29)
    guess = guess - (jnp.left_shift(jnp.ones_like(guess), guess) > value).astype(jnp.int32)
    guess = guess + (jnp.left_shift(jnp.ones_like(guess), guess + 1) <= value).astype(jnp.int32)
    return jnp.clip(guess, 0, bucket_total - 1)


def lookup(table, index_rows, table_len):
    chosen = (index_rows[:, None] == jnp.arange(table_len, dtype=jnp.int32)[None, :]).astype(
        jnp.int32
    )
    return jnp.sum(chosen * table[None, :], axis=1)


def live_of(query_info, key_info):
    query_pos, query_hist, query_valid, query_inv = query_info
    key_pos, key_hist, key_valid, key_inv = key_info
    live_mask = (query_hist[:, None] == key_hist[None, :]) & (
        key_pos[None, :] <= query_pos[:, None]
    )
    return live_mask & query_valid[:, None] & key_valid[None, :]


def pair_core(
    query_part, key_part, value_part, cotan_part, query_info, key_info, rab_table, score_scale
):
    live_f = live_of(query_info, key_info).astype(jnp.float32)
    query_inv = query_info[3]
    bucket = bucket_of(
        jnp.maximum(query_info[0][:, None] - key_info[0][None, :], 0), rab_table.shape[1]
    )
    score_bias = jnp.take(rab_table, bucket, axis=1)
    scores = (
        jnp.einsum("ihd,jhd->hij", query_part, key_part, preferred_element_type=jnp.float32)
        * score_scale
        + score_bias
    )
    sigmoid_s = jax.nn.sigmoid(scores)
    attn = scores * sigmoid_s * live_f * query_inv[None, :, None]
    grad_attn = (
        jnp.einsum("ihd,jhd->hij", cotan_part, value_part, preferred_element_type=jnp.float32)
        * live_f
        * query_inv[None, :, None]
    )
    grad_score = grad_attn * (sigmoid_s * (1.0 + scores * (1.0 - sigmoid_s)))
    return (attn, grad_score, bucket)


def bias_terms(grad_score, bucket, bucket_total):
    one_hot = (
        bucket.reshape(-1)[:, None] == jnp.arange(bucket_total, dtype=jnp.int32)[None, :]
    ).astype(jnp.float32)
    flat_grad = grad_score.reshape(grad_score.shape[0], -1)
    return jnp.dot(
        flat_grad, one_hot, precision=lax.Precision.HIGHEST, preferred_element_type=jnp.float32
    )


def per_device(
    queries, key_rows, value_rows, grad_out, rab_table, first_block, block_fill, block_order
):
    row_count, feat_width = queries.shape
    head_count, bucket_total = rab_table.shape
    head_dim = feat_width // head_count
    score_scale = head_dim ** (-0.5)
    block_total = first_block.shape[1]
    head_block = first_block[0]
    fill_count = block_fill[0]
    slot_order = block_order[0]
    same_hist = (head_block[:, None] == head_block[None, :]).astype(jnp.int32)
    hist_len = jnp.sum(same_hist * fill_count[None, :], axis=1)
    slot_hist = lookup(head_block, slot_order, block_total)
    slot_fill = lookup(fill_count, slot_order, block_total)
    slot_len = lookup(hist_len, slot_order, block_total)

    def make_info(offset, count_rows):
        row_ids = offset + jnp.arange(count_rows, dtype=jnp.int32)
        slot_ids = row_ids // row_count
        within = row_ids - slot_ids * row_count
        logical = lookup(slot_order, slot_ids, block_total)
        positions = logical * row_count + within
        hist_ids = lookup(slot_hist, slot_ids, block_total)
        valid_rows = within < lookup(slot_fill, slot_ids, block_total)
        inverse_len = 1.0 / lookup(slot_len, slot_ids, block_total).astype(jnp.float32)
        return (positions, hist_ids, valid_rows, inverse_len)

    own_info = make_info(lax.axis_index("ctx") * row_count, row_count)
    own_query = queries.reshape(row_count, head_count, head_dim)
    own_key = key_rows.reshape(row_count, head_count, head_dim)
    own_value = value_rows.reshape(row_count, head_count, head_dim)
    own_cotan = grad_out.reshape(row_count, head_count, head_dim)

    def query_side(state, piece_key, piece_value, info):
        count_rows = piece_key.shape[0]
        key_part = piece_key.reshape(count_rows, head_count, head_dim)
        value_part = piece_value.reshape(count_rows, head_count, head_dim)
        query_total, rab_total = state
        attn, grad_score, bucket = pair_core(
            own_query, key_part, value_part, own_cotan, own_info, info, rab_table, score_scale
        )
        score_low = grad_score.astype(jnp.bfloat16)
        query_grad = (
            jnp.einsum("hij,jhd->ihd", score_low, key_part, preferred_element_type=jnp.float32)
            * score_scale
        )
        rab_terms = bias_terms(grad_score, bucket, bucket_total)
        return (query_total + query_grad.reshape(row_count, feat_width), rab_total + rab_terms)

    def key_side(state, piece_query, piece_cotan, info):
        count_rows = piece_query.shape[0]
        query_part = piece_query.reshape(count_rows, head_count, head_dim)
        cotan_part = piece_cotan.reshape(count_rows, head_count, head_dim)
        key_total, value_total = state
        attn, grad_score, bucket = pair_core(
            query_part, own_key, own_value, cotan_part, info, own_info, rab_table, score_scale
        )
        key_grad = (
            jnp.einsum(
                "hij,ihd->jhd",
                grad_score.astype(jnp.bfloat16),
                query_part,
                preferred_element_type=jnp.float32,
            )
            * score_scale
        )
        value_grad = jnp.einsum(
            "hij,ihd->jhd",
            attn.astype(jnp.bfloat16),
            cotan_part,
            preferred_element_type=jnp.float32,
        )
        return (
            key_total + key_grad.reshape(row_count, feat_width),
            value_total + value_grad.reshape(row_count, feat_width),
        )

    zero_rows = jnp.zeros((row_count, feat_width), jnp.float32)
    zero_rab = jnp.zeros((head_count, bucket_total), jnp.float32)

    def tile_all(totals, tiles, info):
        tile_query, tile_key, tile_value, tile_cotan = tiles
        query_state = query_side((totals[0], totals[1]), tile_key, tile_value, info)
        key_state = key_side((totals[2], totals[3]), tile_query, tile_cotan, info)
        return (query_state[0], query_state[1], key_state[0], key_state[1])

    pieces = (
        lax.all_gather(queries, "ctx", axis=0, tiled=True),
        lax.all_gather(key_rows, "ctx", axis=0, tiled=True),
        lax.all_gather(value_rows, "ctx", axis=0, tiled=True),
        lax.all_gather(grad_out, "ctx", axis=0, tiled=True),
    )
    tile_count = pieces[0].shape[0] // row_count
    stacked = tuple((piece.reshape(tile_count, row_count, feat_width) for piece in pieces))

    def step(carry, item):
        tile_index = item[0]
        info = make_info(tile_index * row_count, row_count)
        return (tile_all(carry, item[1:], info), None)

    result, unused = lax.scan(
        step,
        (zero_rows, zero_rab, zero_rows, zero_rows),
        (jnp.arange(tile_count, dtype=jnp.int32),) + stacked,
    )
    totals = result
    query_total, rab_total, key_total, value_total = totals
    grad_rab = lax.psum(rab_total, ("dp", "ctx"))
    return (
        query_total.astype(jnp.bfloat16),
        key_total.astype(jnp.bfloat16),
        value_total.astype(jnp.bfloat16),
        grad_rab,
    )


def solution(mesh):
    return jax.shard_map(
        per_device,
        mesh=mesh,
        in_specs=(
            P(("dp", "ctx"), None),
            P(("dp", "ctx"), None),
            P(("dp", "ctx"), None),
            P(("dp", "ctx"), None),
            P(),
            P("dp", None),
            P("dp", None),
            P("dp", None),
        ),
        out_specs=(P(("dp", "ctx"), None), P(("dp", "ctx"), None), P(("dp", "ctx"), None), P()),
        check_vma=False,
    )
```

profile of v0, /device:TPU:0, one launch (start us, length us, event | category | flops | bytes accessed | tf_op | source)
XLA Modules:
  0.0 2158.5 jit_solution(11833591933152048260)
XLA Ops:
  19.4 1.5 select_reduce_fusion.8
  22.8 6.2 all-gather.5.cloned.1.call-done
  29.0 18.3 all-gather.7.cloned.1.call-done
  47.3 18.3 all-gather.9.cloned.1.call-done
  65.7 18.2 all-gather.11.cloned.1.call-done
  84.4 2022.4 %while.19 = (s32[]{:T(128)}, f32[256,512]{0,1:T(8,128)}, f32[4,13]{1,0:T(4,128)}, f32[256,512]{0,1:T(8,128)}, f32[256,512]{0,1:T(8,128)}, /*index=5*/bf16[4,256,...) while((s32[]{:T(128)}, f32[256,512]{0,1:T(8,128)}, ...), condition=%wide.region_13.15_spmd.clone, body=%wide.region_8.14_spmd.clone.sunk | while | flops 529553760 | bytes 60708524 | solution.py:168
  88.3 1.4 select_reduce_fusion.13
  91.2 215.5 %gather_fusion = f32[65536,4]{1,0:T(8,128)} fusion(f32[4,13]{0,1:T(8,128)S(1)} %get-tuple-element.793, s32[65536]{0:T(1024)S(1)} %broadcast_clamp_fusion.4), kind=kCustom, calls=%fused_computation.clone.clone.1 | custom fusion | bytes 2359296 | tf_op jit(solution)/shard_map/while/body/eval_jaxpr/jit(_take)/gather | solution.py:40
  306.7 18.8 copy.212
  325.5 2.4 and_convert_fusion.3
  327.9 2.4 subtract_multiply_fusion.2
  330.7 1.6 copy.214
  332.2 1.8 copy.215
  334.0 1.5 fusion.77
  340.0 3.3 fusion.78
  346.4 215.5 %gather_fusion.1 = f32[65536,4]{1,0:T(8,128)} fusion(f32[4,13]{0,1:T(8,128)S(1)} %get-tuple-element.793, s32[65536]{0:T(1024)S(1)} %broadcast_clamp_fusion.5), kind=kCustom, calls=%fused_computation.1.clone.clone.1 | custom fusion | bytes 2359296 | tf_op jit(solution)/shard_map/while/body/eval_jaxpr/jit(_take)/gather | solution.py:40
  561.9 19.0 copy.222
  584.1 1.5 fusion.80
  585.6 1.8 fusion.81
  592.6 1.4 select_reduce_fusion.13
  595.5 215.5 %gather_fusion = f32[65536,4]{1,0:T(8,128)} fusion(f32[4,13]{0,1:T(8,128)S(1)} %get-tuple-element.793, s32[65536]{0:T(1024)S(1)} %broadcast_clamp_fusion.4), kind=kCustom, calls=%fused_computation.clone.clone.1 | custom fusion | bytes 2359296 | tf_op jit(solution)/shard_map/while/body/eval_jaxpr/jit(_take)/gather | solution.py:40
  811.0 18.8 copy.212
  829.8 2.4 and_convert_fusion.3
  832.2 2.4 subtract_multiply_fusion.2
  835.0 1.6 copy.214
  836.6 1.8 copy.215
  838.3 1.5 fusion.77
  841.0 1.9 bitcast_add_fusion.5
  845.3 3.9 fusion.78
  852.4 215.5 %gather_fusion.1 = f32[65536,4]{1,0:T(8,128)} fusion(f32[4,13]{0,1:T(8,128)S(1)} %get-tuple-element.793, s32[65536]{0:T(1024)S(1)} %broadcast_clamp_fusion.5), kind=kCustom, calls=%fused_computation.1.clone.clone.1 | custom fusion | bytes 2359296 | tf_op jit(solution)/shard_map/while/body/eval_jaxpr/jit(_take)/gather | solution.py:40
  1067.9 19.0 copy.222
  1090.1 1.5 fusion.80
  1091.6 1.8 fusion.81
  1098.7 1.4 select_reduce_fusion.13
  1101.5 215.5 %gather_fusion = f32[65536,4]{1,0:T(8,128)} fusion(f32[4,13]{0,1:T(8,128)S(1)} %get-tuple-element.793, s32[65536]{0:T(1024)S(1)} %broadcast_clamp_fusion.4), kind=kCustom, calls=%fused_computation.clone.clone.1 | custom fusion | bytes 2359296 | tf_op jit(solution)/shard_map/while/body/eval_jaxpr/jit(_take)/gather | solution.py:40
  1317.0 18.8 copy.212
  1335.9 2.4 and_convert_fusion.3
  1338.2 2.4 subtract_multiply_fusion.2
  1341.0 1.6 copy.214
  1342.6 1.8 copy.215
  1344.4 1.5 fusion.77
  1347.1 1.9 bitcast_add_fusion.5
  1351.4 3.9 fusion.78
  1358.4 215.5 %gather_fusion.1 = f32[65536,4]{1,0:T(8,128)} fusion(f32[4,13]{0,1:T(8,128)S(1)} %get-tuple-element.793, s32[65536]{0:T(1024)S(1)} %broadcast_clamp_fusion.5), kind=kCustom, calls=%fused_computation.1.clone.clone.1 | custom fusion | bytes 2359296 | tf_op jit(solution)/shard_map/while/body/eval_jaxpr/jit(_take)/gather | solution.py:40
  1573.9 19.0 copy.222
  1596.1 1.5 fusion.80
  1597.6 1.8 fusion.81
  1607.5 215.5 %gather_fusion = f32[65536,4]{1,0:T(8,128)} fusion(f32[4,13]{0,1:T(8,128)S(1)} %get-tuple-element.793, s32[65536]{0:T(1024)S(1)} %broadcast_clamp_fusion.4), kind=kCustom, calls=%fused_computation.clone.clone.1 | custom fusion | bytes 2359296 | tf_op jit(solution)/shard_map/while/body/eval_jaxpr/jit(_take)/gather | solution.py:40
  1823.0 18.8 copy.212
  1841.9 2.4 and_convert_fusion.3
  1844.3 2.4 subtract_multiply_fusion.2
  1847.0 1.6 copy.214
  1848.6 1.8 copy.215
  1850.4 1.5 fusion.77
  1853.1 1.9 bitcast_add_fusion.5
  1857.4 3.9 fusion.78
  1864.4 215.5 %gather_fusion.1 = f32[65536,4]{1,0:T(8,128)} fusion(f32[4,13]{0,1:T(8,128)S(1)} %get-tuple-element.793, s32[65536]{0:T(1024)S(1)} %broadcast_clamp_fusion.5), kind=kCustom, calls=%fused_computation.1.clone.clone.1 | custom fusion | bytes 2359296 | tf_op jit(solution)/shard_map/while/body/eval_jaxpr/jit(_take)/gather | solution.py:40
  2079.9 19.0 copy.222
  2102.2 1.5 fusion.80
  2103.7 1.8 fusion.81
  2106.8 1.9 copy.169
  2108.6 1.9 copy.170
  2110.5 1.9 copy.171
  2112.4 39.6 %psum.7 = f32[4,13]{1,0:T(4,128)} all-reduce(f32[4,13]{1,0:T(4,128)} %get-tuple-element.293), channel_id=1, replica_groups=mesh['dp'=8,'ctx'=4] {'dp','ctx'}, use_global_device_ids=true, to_apply=%region_14.16 | all-reduce | flops 52 | bytes 416 | tf_op jit(solution)/shard_map/psum | solution.py:175
  (186 shorter events, 81.2 us)
Async XLA Ops:
  7.2 21.8 %all-gather.5.cloned.1.call-start = ((), (), s32[]{:S(2)}) async-start(), calls=%async_computation | async-start | bytes 1310720 | tf_op jit(solution)/shard_map/all_gather | solution.py:156
  7.9 39.4 %all-gather.7.cloned.1.call-start = ((), (), s32[]{:S(2)}) async-start(), calls=%async_computation.1 | async-start | bytes 1310720 | tf_op jit(solution)/shard_map/all_gather | solution.py:157
  8.6 57.0 %all-gather.9.cloned.1.call-start = ((), (), s32[]{:S(2)}) async-start(), calls=%async_computation.2 | async-start | bytes 1310720 | tf_op jit(solution)/shard_map/all_gather | solution.py:155
  9.4 74.4 %all-gather.11.cloned.1.call-start = ((), (), s32[]{:S(2)}) async-start(), calls=%async_computation.3 | async-start | bytes 1310720 | tf_op jit(solution)/shard_map/all_gather | solution.py:158
  85.6 246.7 %copy-start = (bf16[1,256,512]{1,2,0:T(8,128)(2,1)}, bf16[1,256,512]{1,2,0:T(8,128)(2,1)S(1)}, u32[]{:S(2)}) copy-start(bf16[1,256,512]{1,2,0:T(8,128)(2,1)S(1)} %copy.209) | copy-start | bytes 786436 | tf_op jit(solution)/shard_map/while
  338.0 249.4 %copy-start.1 = (f32[256,512]{0,1:T(8,128)S(1)}, f32[256,512]{0,1:T(8,128)}, u32[]{:S(2)}) copy-start(f32[256,512]{0,1:T(8,128)} %get-tuple-element.753) | copy-start | bytes 1572868 | tf_op jit(solution)/shard_map/while
  338.0 249.4 %copy-start.3 = (f32[256,512]{0,1:T(8,128)S(1)}, f32[256,512]{0,1:T(8,128)}, u32[]{:S(2)}) copy-start(f32[256,512]{0,1:T(8,128)} %get-tuple-element.754) | copy-start | bytes 1572868 | tf_op jit(solution)/shard_map/while
  584.1 1.5 copy-start.5
  587.7 0.8 copy-start.2
  587.7 1.0 copy-start.4
  589.9 246.7 %copy-start = (bf16[1,256,512]{1,2,0:T(8,128)(2,1)}, bf16[1,256,512]{1,2,0:T(8,128)(2,1)S(1)}, u32[]{:S(2)}) copy-start(bf16[1,256,512]{1,2,0:T(8,128)(2,1)S(1)} %copy.209) | copy-start | bytes 786436 | tf_op jit(solution)/shard_map/while
  843.3 250.1 %copy-start.1 = (f32[256,512]{0,1:T(8,128)S(1)}, f32[256,512]{0,1:T(8,128)}, u32[]{:S(2)}) copy-start(f32[256,512]{0,1:T(8,128)} %get-tuple-element.753) | copy-start | bytes 1572868 | tf_op jit(solution)/shard_map/while
  843.3 250.1 %copy-start.3 = (f32[256,512]{0,1:T(8,128)S(1)}, f32[256,512]{0,1:T(8,128)}, u32[]{:S(2)}) copy-start(f32[256,512]{0,1:T(8,128)} %get-tuple-element.754) | copy-start | bytes 1572868 | tf_op jit(solution)/shard_map/while
  1090.1 1.5 copy-start.5
  1093.7 0.8 copy-start.2
  1093.7 1.0 copy-start.4
  1095.9 246.7 %copy-start = (bf16[1,256,512]{1,2,0:T(8,128)(2,1)}, bf16[1,256,512]{1,2,0:T(8,128)(2,1)S(1)}, u32[]{:S(2)}) copy-start(bf16[1,256,512]{1,2,0:T(8,128)(2,1)S(1)} %copy.209) | copy-start | bytes 786436 | tf_op jit(solution)/shard_map/while
  1349.3 250.1 %copy-start.1 = (f32[256,512]{0,1:T(8,128)S(1)}, f32[256,512]{0,1:T(8,128)}, u32[]{:S(2)}) copy-start(f32[256,512]{0,1:T(8,128)} %get-tuple-element.753) | copy-start | bytes 1572868 | tf_op jit(solution)/shard_map/while
  1349.3 250.1 %copy-start.3 = (f32[256,512]{0,1:T(8,128)S(1)}, f32[256,512]{0,1:T(8,128)}, u32[]{:S(2)}) copy-start(f32[256,512]{0,1:T(8,128)} %get-tuple-element.754) | copy-start | bytes 1572868 | tf_op jit(solution)/shard_map/while
  1596.1 1.5 copy-start.5
  1599.7 0.8 copy-start.2
  1599.8 1.0 copy-start.4
  1601.9 246.7 %copy-start = (bf16[1,256,512]{1,2,0:T(8,128)(2,1)}, bf16[1,256,512]{1,2,0:T(8,128)(2,1)S(1)}, u32[]{:S(2)}) copy-start(bf16[1,256,512]{1,2,0:T(8,128)(2,1)S(1)} %copy.209) | copy-start | bytes 786436 | tf_op jit(solution)/shard_map/while
  1855.4 250.1 %copy-start.1 = (f32[256,512]{0,1:T(8,128)S(1)}, f32[256,512]{0,1:T(8,128)}, u32[]{:S(2)}) copy-start(f32[256,512]{0,1:T(8,128)} %get-tuple-element.753) | copy-start | bytes 1572868 | tf_op jit(solution)/shard_map/while
  1855.4 250.1 %copy-start.3 = (f32[256,512]{0,1:T(8,128)S(1)}, f32[256,512]{0,1:T(8,128)}, u32[]{:S(2)}) copy-start(f32[256,512]{0,1:T(8,128)} %get-tuple-element.754) | copy-start | bytes 1572868 | tf_op jit(solution)/shard_map/while
  2102.1 1.5 copy-start.5
  2105.8 0.8 copy-start.2
  2105.8 1.0 copy-start.4
Sparse Core Ops, SparseCore 0:
  9.6 19.4 all-gather.4
  30.6 16.7 all-gather.6
  48.9 16.7 all-gather.8
  67.1 16.7 all-gather.10
where the time goes:
time: 2160 us
  local copies, waits for them, and re-layouts  1950 us (90%)
  waiting for transfers between devices  63.6 us (3%)
  matrix products  53.8 us (2%)
  blocking collectives  39.6 us (2%)
  other arithmetic  36.1 us (2%)
    gather x16, local copies, waits for them, and re-layouts, pair_core(): score_bias = jnp.take(rab_table, bucket, axis=1)  1880 us
  transfers between devices with their start and end apart: 4, of which 4 were waited for; matrix products, arithmetic and copies ran while one was open for 1% of the time, Pallas kernels for 0%

commit v1 on v0

--- a/solution.py
+++ b/solution.py
@@ -1,7 +1,361 @@
+import functools
+
 import jax
 import jax.numpy as jnp
 from jax import lax
+from jax.experimental import pallas as pl
+from jax.experimental.pallas import tpu as pltpu
 from jax.sharding import PartitionSpec as P
+
+MESH = pl.DeviceIdType.MESH
+F32 = jnp.float32
+BF16 = jnp.bfloat16
+
+
+def bucket_count(distance, bucket_total):
+    value = distance + 1
+    result = jnp.zeros(distance.shape, jnp.int32)
+    for power in range(1, bucket_total):
+        result = result + jnp.where(value >= 2**power, 1, 0).astype(jnp.int32)
+    return result
+
+
+def dot_nt(a, b):
+    return lax.dot_general(a, b, (((1,), (1,)), ((), ())), preferred_element_type=F32)
+
+
+def dot_nn(a, b):
+    return lax.dot_general(a, b, (((1,), (0,)), ((), ())), preferred_element_type=F32)
+
+
+def dot_tn(a, b):
+    return lax.dot_general(a, b, (((0,), (0,)), ((), ())), preferred_element_type=F32)
+
+
+def fused_kernel(
+    n_dp,
+    head_count,
+    bucket_total,
+    order_ref,
+    first_ref,
+    fill_ref,
+    q_ref,
+    k_ref,
+    v_ref,
+    d_ref,
+    table_ref,
+    gq_ref,
+    gk_ref,
+    gv_ref,
+    rab_ref,
+    vm,
+    dm,
+    send1,
+    send2,
+    base2,
+    recv1,
+    recv2,
+    recv3,
+    accq,
+    acck,
+    accv,
+    biasv,
+    rabs,
+    ctx_slots,
+    dp_slots,
+    s1_send,
+    s1_recv,
+    s2_send,
+    s2_recv,
+    s3_send,
+    s3_recv,
+    rc_send,
+    rc_recv,
+    rd_send,
+    rd_recv,
+):
+    rows = q_ref.shape[0]
+    dim = q_ref.shape[1] // head_count
+    scale = dim ** (-0.5)
+    blocks = 4
+    dp = lax.axis_index("dp")
+    me = lax.axis_index("ctx")
+    sib = me + 1 - 2 * (me % 2)
+    cross = (me + 2) % 4
+    diag = (sib + 2) % 4
+
+    barrier = pltpu.get_barrier_semaphore()
+    for step in range(1, blocks):
+        pl.semaphore_signal(barrier, inc=1, device_id=(dp, (me + step) % blocks), device_id_type=MESH)
+    for step in range(1, n_dp):
+        pl.semaphore_signal(barrier, inc=1, device_id=((dp + step) % n_dp, me), device_id_type=MESH)
+
+    last = blocks - 1
+    log_me = order_ref[0, me]
+    log_sib = order_ref[0, sib]
+    log_cross = order_ref[0, cross]
+    log_diag = order_ref[0, diag]
+    hist_me = first_ref[0, log_me]
+    fill_me = fill_ref[0, log_me]
+    length = jnp.int32(0)
+    for block in range(blocks):
+        length = length + jnp.where(first_ref[0, block] == hist_me, fill_ref[0, block], 0)
+    inverse = 1.0 / jnp.full((1, rows), length, jnp.int32).astype(F32)
+
+    idle = log_me == last
+    with_idle = idle | (log_sib == last)
+
+    row_wide = lax.broadcasted_iota(jnp.int32, (rows, dim), 0)
+    row_ok = jnp.where(row_wide < fill_me, 1.0, 0.0).astype(F32).astype(BF16)
+
+    def cols(h):
+        return pl.ds(pl.multiple_of(h * dim, dim), dim)
+
+    log_one = jnp.where(log_sib == last, log_diag, log_sib)
+    log_two = jnp.where(log_cross == last, log_diag, log_cross)
+    early_one = log_me < log_one
+    early_two = log_me < log_two
+
+    def prepare(h, carry):
+        at = cols(h)
+        q_h, k_h = q_ref[:, at], k_ref[:, at]
+        v_h, d_h = v_ref[:, at] * row_ok, d_ref[:, at] * row_ok
+        vm[:, at] = v_h
+        dm[:, at] = d_h
+        send1[h, 0] = jnp.where(early_one, k_h, q_h)
+        send1[h, 1] = jnp.where(early_one, v_h, d_h)
+        base2[h, 0] = jnp.where(early_two, k_h, q_h)
+        base2[h, 1] = jnp.where(early_two, v_h, d_h)
+        return carry
+
+    lax.fori_loop(0, head_count, prepare, 0)
+
+    pl.semaphore_wait(barrier, blocks - 1 + n_dp - 1)
+
+    def copy1(h):
+        return pltpu.make_async_remote_copy(
+            src_ref=send1.at[h], dst_ref=recv1.at[h], send_sem=s1_send.at[h], recv_sem=s1_recv.at[h],
+            device_id=(dp, sib), device_id_type=MESH)
+
+    def copy2(h):
+        return pltpu.make_async_remote_copy(
+            src_ref=send2.at[h], dst_ref=recv2.at[h], send_sem=s2_send.at[h], recv_sem=s2_recv.at[h],
+            device_id=(dp, cross), device_id_type=MESH)
+
+    def copy3(h):
+        return pltpu.make_async_remote_copy(
+            src_ref=recv2.at[h], dst_ref=recv3.at[h], send_sem=s3_send.at[h], recv_sem=s3_recv.at[h],
+            device_id=(dp, sib), device_id_type=MESH)
+
+    for h in range(head_count):
+        copy1(h).start()
+
+    table = table_ref[...]
+    lane = lax.broadcasted_iota(jnp.int32, (head_count, 2 * rows), 1)
+    offset = jnp.where(lane < rows, -lane, 2 * rows - lane)
+
+    def distance_of(delta):
+        return jnp.abs(delta * rows + offset)
+
+    log_a = jnp.where(with_idle, log_diag, log_sib)
+    log_b = log_two
+    delta_a, delta_b = log_me - log_a, log_me - log_b
+    buckets = (
+        bucket_count(jnp.maximum(offset, 0), bucket_total),
+        bucket_count(distance_of(delta_a), bucket_total),
+        bucket_count(distance_of(delta_b), bucket_total),
+    )
+    for kind in range(3):
+        filled = jnp.zeros((head_count, 2 * rows), F32)
+        for b in range(bucket_total):
+            filled = jnp.where(buckets[kind] == b, table[:, b : b + 1], filled)
+        for h in range(head_count):
+            biasv[kind, h] = filled[h : h + 1] * 0.5
+
+    for h in range(head_count):
+        copy1(h).wait_recv()
+        send2[h] = jnp.where(idle, recv1[h], base2[h])
+        copy2(h).start()
+
+    i_row = lax.broadcasted_iota(jnp.int32, (rows, rows), 0)
+    j_col = lax.broadcasted_iota(jnp.int32, (rows, rows), 1)
+
+    def bias_of(kind, h):
+        spread = jnp.broadcast_to(biasv[kind, h], (rows, 2 * rows))
+        return pltpu.roll(spread, 0, 1, stride=1, stride_axis=0)[:, :rows]
+
+    lane8 = lax.broadcasted_iota(jnp.int32, (8, rows), 1)
+
+    def by_offset(grad_score):
+        low = jnp.zeros((8, rows), F32)
+        high = jnp.zeros((8, rows), F32)
+        for start in range(0, rows, 8):
+            part = grad_score[start : start + 8, :]
+            if start == 0:
+                low = low + part
+            else:
+                turned = pltpu.roll(part, rows - start, 1)
+                wrapped = lane8 >= rows - start
+                low = low + jnp.where(wrapped, 0.0, turned)
+                high = high + jnp.where(wrapped, turned, 0.0)
+        return low, high
+
+    def pair_terms(score_dot, grad_dot, bias, factor):
+        half = score_dot * (scale * 0.5) + bias
+        turn = jnp.tanh(half)
+        up = 1.0 + turn
+        raw = half * up
+        attn = raw * factor
+        slope = (up + raw * (1.0 - turn)) * (factor * 0.5)
+        return attn.astype(BF16), grad_dot * slope
+
+    def own_pair(h):
+        at = cols(h)
+        q_h, k_h, v_h, d_h = q_ref[:, at], k_ref[:, at], vm[:, at], dm[:, at]
+        factor = jnp.where(j_col <= i_row, inverse, 0.0)
+        attn, grad_score = pair_terms(dot_nt(q_h, k_h), dot_nt(d_h, v_h), bias_of(0, h), factor)
+        low_score = grad_score.astype(BF16)
+        accq[h] = dot_nn(low_score, k_h)
+        acck[h] = dot_tn(low_score, q_h)
+        accv[h] = dot_tn(attn, d_h)
+        low, high = by_offset(grad_score)
+        rabs[0, h, :, :rows] = low
+        rabs[0, h, :, rows:] = high
+
+    def other_pair(kind, h, part0, part1, delta, factor):
+        at = cols(h)
+        later = delta > 0
+        own0 = jnp.where(later, q_ref[:, at], k_ref[:, at])
+        own1 = jnp.where(later, dm[:, at], vm[:, at])
+        attn, grad_score = pair_terms(dot_nt(own0, part0), dot_nt(own1, part1), bias_of(kind, h), factor)
+        term0 = dot_nn(grad_score.astype(BF16), part0)
+        term1 = dot_nn(attn, part1)
+        low, high = by_offset(grad_score)
+        take = jnp.where(later, 1.0, 0.0)
+        rabs[kind, h, :, :rows] = low * take
+        rabs[kind, h, :, rows:] = high * take
+        return jnp.where(later, term0, 0.0), jnp.where(later, 0.0, term0), jnp.where(later, 0.0, term1)
+
+    factor_a = jnp.where(first_ref[0, log_a] == hist_me, inverse, 0.0)
+    factor_b = jnp.where(first_ref[0, log_b] == hist_me, inverse, 0.0)
+    factor_a = jnp.where(idle, 0.0, factor_a)
+    factor_b = jnp.where(idle, 0.0, factor_b)
+
+    def own_step(h, carry):
+        own_pair(h)
+        return carry
+
+    lax.fori_loop(0, head_count, own_step, 0)
+
+    def other_step(h, carry):
+        at = cols(h)
+        copy2(h).wait_recv()
+        copy3(h).start()
+        q_b, k_b, v_b = other_pair(2, h, recv2[h, 0], recv2[h, 1], delta_b, factor_b)
+        copy3(h).wait_recv()
+        part0 = jnp.where(with_idle, recv3[h, 0], recv1[h, 0])
+        part1 = jnp.where(with_idle, recv3[h, 1], recv1[h, 1])
+        q_a, k_a, v_a = other_pair(1, h, part0, part1, delta_a, factor_a)
+        ok = row_wide < fill_me
+        gq_ref[:, at] = ((accq[h] + q_a + q_b) * scale).astype(BF16)
+        gk_ref[:, at] = ((acck[h] + k_a + k_b) * scale).astype(BF16)
+        gv_ref[:, at] = jnp.where(ok, accv[h] + v_a + v_b, 0.0).astype(BF16)
+        return carry
+
+    lax.fori_loop(0, head_count, other_step, 0)
+
+    lane_out = lax.broadcasted_iota(jnp.int32, (head_count, 128), 1)
+    lane_sum = lax.broadcasted_iota(jnp.int32, (8, 2 * rows), 1)
+    offset_sum = lax.broadcasted_iota(jnp.int32, (8, 2 * rows), 0) - jnp.where(
+        lane_sum < rows, lane_sum, lane_sum - 2 * rows
+    )
+    sum_buckets = (
+        bucket_count(jnp.maximum(offset_sum, 0), bucket_total),
+        bucket_count(jnp.abs(delta_a * rows + offset_sum), bucket_total),
+        bucket_count(jnp.abs(delta_b * rows + offset_sum), bucket_total),
+    )
+    mine = jnp.zeros((head_count, 128), F32)
+    for b in range(bucket_total):
+        here = [sum_buckets[kind] == b for kind in range(3)]
+        per_head = []
+        for h in range(head_count):
+            picked = jnp.zeros((8, 2 * rows), F32)
+            for kind in range(3):
+                picked = picked + jnp.where(here[kind], rabs[kind, h], 0.0)
+            per_head.append(jnp.sum(picked, axis=0, keepdims=True))
+        sums = jnp.sum(jnp.concatenate(per_head, axis=0), axis=1, keepdims=True)
+        mine = jnp.where(lane_out == b, sums, mine)
+    ctx_slots[me] = jnp.concatenate([mine, jnp.zeros((8 - head_count, 128), F32)], axis=0)
+
+    def rab_ctx(step, owner):
+        return pltpu.make_async_remote_copy(
+            src_ref=ctx_slots.at[owner], dst_ref=ctx_slots.at[owner], send_sem=rc_send.at[step],
+            recv_sem=rc_recv.at[owner], device_id=(dp, (me + step) % blocks), device_id_type=MESH)
+
+    def rab_dp(step, owner):
+        return pltpu.make_async_remote_copy(
+            src_ref=dp_slots.at[owner], dst_ref=dp_slots.at[owner], send_sem=rd_send.at[step],
+            recv_sem=rd_recv.at[owner], device_id=((dp + step) % n_dp, me), device_id_type=MESH)
+
+    for step in range(1, blocks):
+        rab_ctx(step, me).start()
+    for step in range(1, blocks):
+        rab_ctx(step, (me + step) % blocks).wait_recv()
+    total = ctx_slots[0]
+    for slot in range(1, blocks):
+        total = total + ctx_slots[slot]
+    dp_slots[dp] = total
+    for step in range(1, n_dp):
+        rab_dp(step, dp).start()
+    for h in range(head_count):
+        copy1(h).wait_send()
+        copy2(h).wait_send()
+        copy3(h).wait_send()
+    for step in range(1, blocks):
+        rab_ctx(step, me).wait_send()
+    for step in range(1, n_dp):
+        rab_dp(step, (dp + step) % n_dp).wait_recv()
+    total = dp_slots[0]
+    for slot in range(1, n_dp):
+        total = total + dp_slots[slot]
+    for step in range(1, n_dp):
+        rab_dp(step, dp).wait_send()
+    rab_ref[...] = total[:head_count, :bucket_total]
+
+
+def four_block_device(
+    n_dp, queries, key_rows, value_rows, grad_out, rab_table, first_block, block_fill, block_order
+):
+    rows, width = queries.shape
+    heads, bucket_total = rab_table.shape
+    dim = width // heads
+    vmem = pl.BlockSpec(memory_space=pltpu.VMEM)
+    smem = pl.BlockSpec(memory_space=pltpu.SMEM)
+    out = jax.ShapeDtypeStruct((rows, width), BF16)
+    buf = pltpu.VMEM((heads, 2, rows, dim), BF16)
+    acc = pltpu.VMEM((heads, rows, dim), F32)
+    dma = pltpu.SemaphoreType.DMA
+    return pl.pallas_call(
+        functools.partial(fused_kernel, n_dp, heads, bucket_total),
+        out_shape=(out, out, out, jax.ShapeDtypeStruct((heads, bucket_total), F32)),
+        in_specs=[smem] * 3 + [vmem] * 5,
+        out_specs=(vmem,) * 4,
+        scratch_shapes=[
+            pltpu.VMEM((rows, width), BF16),
+            pltpu.VMEM((rows, width), BF16),
+            buf, buf, buf, buf, buf, buf,
+            acc, acc, acc,
+            pltpu.VMEM((3, heads, 1, 2 * rows), F32),
+            pltpu.VMEM((3, heads, 8, 2 * rows), F32),
+            pltpu.VMEM((4, 8, 128), F32),
+            pltpu.VMEM((n_dp, 8, 128), F32),
+            dma((heads,)), dma((heads,)), dma((heads,)), dma((heads,)), dma((heads,)), dma((heads,)),
+            dma((4,)), dma((4,)), dma((n_dp,)), dma((n_dp,)),
+        ],
+        compiler_params=pltpu.CompilerParams(
+            collective_id=0, has_side_effects=True, vmem_limit_bytes=40 * 1024 * 1024
+        ),
+    )(block_order, first_block, block_fill, queries, key_rows, value_rows, grad_out, rab_table)
 
 
 def bucket_of(distance, bucket_total):
@@ -64,7 +418,7 @@
     )
 
 
-def per_device(
+def scan_device(
     queries, key_rows, value_rows, grad_out, rab_table, first_block, block_fill, block_order
 ):
     row_count, feat_width = queries.shape
@@ -182,8 +536,12 @@
 
 
 def solution(mesh):
+    if mesh.shape["ctx"] == 4:
+        body = functools.partial(four_block_device, mesh.shape["dp"])
+    else:
+        body = scan_device
     return jax.shard_map(
-        per_device,
+        body,
         mesh=mesh,
         in_specs=(
             P(("dp", "ctx"), None),

time: 2160 us -> 38.9 us (0.02)
  local copies, waits for them, and re-layouts: 1950 us -> 9.12 us
  waiting for transfers between devices: 63.6 us -> 0 us
  matrix products: 53.8 us -> 0 us
  blocking collectives: 39.6 us -> 0 us
  other arithmetic: 36.1 us -> 0 us
  Pallas kernels: 0 us -> 28.8 us
    gather x16 -> x0, local copies, waits for them, and re-layouts: 1880 us -> none  [pair_core(): score_bias = jnp.take(rab_table, bucket, axis=1)]
    all_gather x4 -> x0, waiting for transfers between devices: 61 us -> none  [the longest x1 18.3 us: per_device(): lax.all_gather(queries, 'ctx', axis=0, tiled=True)]
    dot_general x28 -> x0, matrix products: 53.8 us -> none  [the longest x4 15.1 us: bias_terms(): jnp.dot(flat_grad, one_hot, precision=lax.Precision.HIGHEST, preferred_el...]
    psum x1 -> x0, blocking collectives: 39.6 us -> none  [per_device(): grad_rab = lax.psum(rab_total, ('dp', 'ctx'))]
    pallas_call x0 -> x1, Pallas kernels: none -> 28.8 us  [four_block_device(): pl.pallas_call(functools.partial(fused_kernel, n_dp, heads, bucket_total)...]
    dynamic_slice x32 -> x0, local copies, waits for them, and re-layouts: 24.7 us -> none  [per_device(): lax.scan(step, (zero_rows, zero_rab, zero_rows, zero_rows), (jnp.arange(t...]
  transfers between devices with their start and end apart: 4 -> 0, of which waited for: 4 -> 0; matrix products, arithmetic and copies ran while one was open for 1% -> 0% of each run, Pallas kernels for 0% -> 0%
where the time goes in v1:
time: 38.9 us; the launch traced here: 38.6 us
  Pallas kernels  28.8 us (74%)
  local copies, waits for them, and re-layouts  9.12 us (23%)
  between operations  0.66 us (2%)
    pallas_call x1, Pallas kernels, four_block_device(): pl.pallas_call(functools.partial(fused_kernel, n_dp, heads, bucket_total)...  28.8 us
    unnamed x20, local copies, waits for them, and re-layouts  9.12 us

profile of v1, /device:TPU:0, one launch (start us, length us, event | category | flops | bytes accessed | tf_op | source)
XLA Modules:
  0.0 38.6 jit_solution(4254988451683145052)
XLA Ops:
  0.6 0.0 copy-start
  0.6 0.9 %copy-done = bf16[256,512]{1,0:T(8,128)(2,1)S(1)} copy-done((bf16[256,512]{1,0:T(8,128)(2,1)S(1)}, bf16[256,512]{1,0:T(8,128)(2,1)}, u32[]{:S(2)}) %copy-start) | copy-done | bytes 262168
  1.6 0.0 copy-start.1
  1.6 0.9 %copy-done.1 = bf16[256,512]{1,0:T(8,128)(2,1)S(1)} copy-done((bf16[256,512]{1,0:T(8,128)(2,1)S(1)}, bf16[256,512]{1,0:T(8,128)(2,1)}, u32[]{:S(2)}) %copy-start.1) | copy-done | bytes 262168
  2.5 0.0 copy-start.2
  2.5 0.9 %copy-done.2 = bf16[256,512]{1,0:T(8,128)(2,1)S(1)} copy-done((bf16[256,512]{1,0:T(8,128)(2,1)S(1)}, bf16[256,512]{1,0:T(8,128)(2,1)}, u32[]{:S(2)}) %copy-start.2) | copy-done | bytes 262168
  3.5 0.0 copy-start.3
  3.5 0.9 %copy-done.3 = bf16[256,512]{1,0:T(8,128)(2,1)S(1)} copy-done((bf16[256,512]{1,0:T(8,128)(2,1)S(1)}, bf16[256,512]{1,0:T(8,128)(2,1)}, u32[]{:S(2)}) %copy-start.3) | copy-done | bytes 262168
  4.4 0.0 copy-start.4
  4.4 0.7 %copy-done.4 = f32[4,13]{1,0:T(4,128)S(1)} copy-done((f32[4,13]{1,0:T(4,128)S(1)}, f32[4,13]{1,0:T(4,128)}, u32[]{:S(2)}) %copy-start.4) | copy-done | bytes 232
  5.1 0.0 copy-start.5
  5.1 0.7 %copy-done.5 = s32[1,4]{1,0:T(1,128)S(1)} copy-done((s32[1,4]{1,0:T(1,128)S(1)}, s32[1,4]{1,0:T(1,128)}, u32[]{:S(2)}) %copy-start.5) | copy-done | bytes 40
  5.8 0.0 copy-start.6
  5.8 0.7 %copy-done.6 = s32[1,4]{1,0:T(1,128)S(1)} copy-done((s32[1,4]{1,0:T(1,128)S(1)}, s32[1,4]{1,0:T(1,128)}, u32[]{:S(2)}) %copy-start.6) | copy-done | bytes 40
  6.4 0.0 copy-start.7
  6.4 0.7 %copy-done.7 = s32[1,4]{1,0:T(1,128)S(1)} copy-done((s32[1,4]{1,0:T(1,128)S(1)}, s32[1,4]{1,0:T(1,128)}, u32[]{:S(2)}) %copy-start.7) | copy-done | bytes 40
  7.1 28.8 %shard_map.111 = (bf16[256,512]{1,0:T(8,128)(2,1)S(1)}, bf16[256,512]{1,0:T(8,128)(2,1)S(1)}, bf16[256,512]{1,0:T(8,128)(2,1)S(1)}, f32[4,13]{1,0:T(4,128)S(1)}) custom-call(s32[1,4]{1,0:T(1,128)S(1)} %copy-done.5, s32[1,4]{1,0:T(1,128)S(1)} %copy-done.6, s32[1,4]{1,0:T(1,128)S(1)} %copy-done.7, bf16[256,512]{1,0:T(8,128)(2,1)S(1)} %copy-done, ...), custom_call_target="tpu_custom_call" | custom-call | tf_op jit(solution)/shard_map/pallas_call | solution.py:338
  35.9 0.7 %copy.16 = bf16[256,512]{1,0:T(8,128)(2,1)} copy(bf16[256,512]{1,0:T(8,128)(2,1)S(1)} %get-tuple-element.8) | data formatting | bytes 524288
  36.6 0.7 %copy.17 = bf16[256,512]{1,0:T(8,128)(2,1)} copy(bf16[256,512]{1,0:T(8,128)(2,1)S(1)} %get-tuple-element.9) | data formatting | bytes 524288
  37.3 0.7 %copy.18 = bf16[256,512]{1,0:T(8,128)(2,1)} copy(bf16[256,512]{1,0:T(8,128)(2,1)S(1)} %get-tuple-element.10) | data formatting | bytes 524288
  38.0 0.6 %copy.19 = f32[4,13]{1,0:T(4,128)} copy(f32[4,13]{1,0:T(4,128)S(1)} %get-tuple-element.11) | data formatting | bytes 416
Async XLA Ops:
  0.6 1.0 %copy-start = (bf16[256,512]{1,0:T(8,128)(2,1)S(1)}, bf16[256,512]{1,0:T(8,128)(2,1)}, u32[]{:S(2)}) copy-start(bf16[256,512]{1,0:T(8,128)(2,1)} %q_ref.1) | copy-start | bytes 786436
  1.6 0.9 %copy-start.1 = (bf16[256,512]{1,0:T(8,128)(2,1)S(1)}, bf16[256,512]{1,0:T(8,128)(2,1)}, u32[]{:S(2)}) copy-start(bf16[256,512]{1,0:T(8,128)(2,1)} %k_ref.1) | copy-start | bytes 786436
  2.5 0.9 %copy-start.2 = (bf16[256,512]{1,0:T(8,128)(2,1)S(1)}, bf16[256,512]{1,0:T(8,128)(2,1)}, u32[]{:S(2)}) copy-start(bf16[256,512]{1,0:T(8,128)(2,1)} %v_ref.1) | copy-start | bytes 786436
  3.5 0.9 %copy-start.3 = (bf16[256,512]{1,0:T(8,128)(2,1)S(1)}, bf16[256,512]{1,0:T(8,128)(2,1)}, u32[]{:S(2)}) copy-start(bf16[256,512]{1,0:T(8,128)(2,1)} %d_ref.1) | copy-start | bytes 786436
  4.4 0.7 %copy-start.4 = (f32[4,13]{1,0:T(4,128)S(1)}, f32[4,13]{1,0:T(4,128)}, u32[]{:S(2)}) copy-start(f32[4,13]{1,0:T(4,128)} %table_ref.1) | copy-start | bytes 628
  5.1 0.7 %copy-start.5 = (s32[1,4]{1,0:T(1,128)S(1)}, s32[1,4]{1,0:T(1,128)}, u32[]{:S(2)}) copy-start(s32[1,4]{1,0:T(1,128)} %order_ref.1) | copy-start | bytes 52
  5.8 0.7 %copy-start.6 = (s32[1,4]{1,0:T(1,128)S(1)}, s32[1,4]{1,0:T(1,128)}, u32[]{:S(2)}) copy-start(s32[1,4]{1,0:T(1,128)} %first_ref.1) | copy-start | bytes 52
  6.4 0.7 %copy-start.7 = (s32[1,4]{1,0:T(1,128)S(1)}, s32[1,4]{1,0:T(1,128)}, u32[]{:S(2)}) copy-start(s32[1,4]{1,0:T(1,128)} %fill_ref.1) | copy-start | bytes 52

commit v2 on v1

--- a/solution.py
+++ b/solution.py
@@ -36,20 +36,27 @@
     n_dp,
     head_count,
     bucket_total,
+    order_hbm,
+    first_hbm,
+    fill_hbm,
+    q_hbm,
+    k_hbm,
+    v_hbm,
+    d_hbm,
+    table_hbm,
+    gq_ref,
+    gk_ref,
+    gv_ref,
+    rab_ref,
     order_ref,
     first_ref,
     fill_ref,
     q_ref,
     k_ref,
-    v_ref,
-    d_ref,
-    table_ref,
-    gq_ref,
-    gk_ref,
-    gv_ref,
-    rab_ref,
     vm,
     dm,
+    table_ref,
+    in_sems,
     send1,
     send2,
     base2,
@@ -74,6 +81,15 @@
     rd_send,
     rd_recv,
 ):
+    fetches = [
+        pltpu.make_async_copy(source, target, in_sems.at[index])
+        for index, (source, target) in enumerate((
+            (order_hbm, order_ref), (first_hbm, first_ref), (fill_hbm, fill_ref), (q_hbm, q_ref),
+            (k_hbm, k_ref), (v_hbm, vm), (d_hbm, dm), (table_hbm, table_ref),
+        ))
+    ]
+    for fetch in fetches:
+        fetch.start()
     rows = q_ref.shape[0]
     dim = q_ref.shape[1] // head_count
     scale = dim ** (-0.5)
@@ -89,6 +105,10 @@
         pl.semaphore_signal(barrier, inc=1, device_id=(dp, (me + step) % blocks), device_id_type=MESH)
     for step in range(1, n_dp):
         pl.semaphore_signal(barrier, inc=1, device_id=((dp + step) % n_dp, me), device_id_type=MESH)
+
+    for fetch in fetches:
+        fetch.wait()
+    pl.semaphore_wait(barrier, blocks - 1 + n_dp - 1)
 
     last = blocks - 1
     log_me = order_ref[0, me]
@@ -116,21 +136,16 @@
     early_one = log_me < log_one
     early_two = log_me < log_two
 
-    def prepare(h, carry):
+    def prepare(h):
         at = cols(h)
         q_h, k_h = q_ref[:, at], k_ref[:, at]
-        v_h, d_h = v_ref[:, at] * row_ok, d_ref[:, at] * row_ok
+        v_h, d_h = vm[:, at] * row_ok, dm[:, at] * row_ok
         vm[:, at] = v_h
         dm[:, at] = d_h
         send1[h, 0] = jnp.where(early_one, k_h, q_h)
         send1[h, 1] = jnp.where(early_one, v_h, d_h)
         base2[h, 0] = jnp.where(early_two, k_h, q_h)
         base2[h, 1] = jnp.where(early_two, v_h, d_h)
-        return carry
-
-    lax.fori_loop(0, head_count, prepare, 0)
-
-    pl.semaphore_wait(barrier, blocks - 1 + n_dp - 1)
 
     def copy1(h):
         return pltpu.make_async_remote_copy(
@@ -147,8 +162,12 @@
             src_ref=recv2.at[h], dst_ref=recv3.at[h], send_sem=s3_send.at[h], recv_sem=s3_recv.at[h],
             device_id=(dp, sib), device_id_type=MESH)
 
-    for h in range(head_count):
+    def prepare_and_send(h, carry):
+        prepare(h)
         copy1(h).start()
+        return carry
+
+    lax.fori_loop(0, head_count, prepare_and_send, 0)
 
     table = table_ref[...]
     lane = lax.broadcasted_iota(jnp.int32, (head_count, 2 * rows), 1)
@@ -330,7 +349,6 @@
     heads, bucket_total = rab_table.shape
     dim = width // heads
     vmem = pl.BlockSpec(memory_space=pltpu.VMEM)
-    smem = pl.BlockSpec(memory_space=pltpu.SMEM)
     out = jax.ShapeDtypeStruct((rows, width), BF16)
     buf = pltpu.VMEM((heads, 2, rows, dim), BF16)
     acc = pltpu.VMEM((heads, rows, dim), F32)
@@ -338,11 +356,18 @@
     return pl.pallas_call(
         functools.partial(fused_kernel, n_dp, heads, bucket_total),
         out_shape=(out, out, out, jax.ShapeDtypeStruct((heads, bucket_total), F32)),
-        in_specs=[smem] * 3 + [vmem] * 5,
+        in_specs=[pl.BlockSpec(memory_space=pltpu.HBM)] * 8,
         out_specs=(vmem,) * 4,
         scratch_shapes=[
+            pltpu.SMEM(block_order.shape, jnp.int32),
+            pltpu.SMEM(first_block.shape, jnp.int32),
+            pltpu.SMEM(block_fill.shape, jnp.int32),
             pltpu.VMEM((rows, width), BF16),
             pltpu.VMEM((rows, width), BF16),
+            pltpu.VMEM((rows, width), BF16),
+            pltpu.VMEM((rows, width), BF16),
+            pltpu.VMEM(rab_table.shape, F32),
+            dma((8,)),
             buf, buf, buf, buf, buf, buf,
             acc, acc, acc,
             pltpu.VMEM((3, heads, 1, 2 * rows), F32),
@@ -353,7 +378,7 @@
             dma((4,)), dma((4,)), dma((n_dp,)), dma((n_dp,)),
         ],
         compiler_params=pltpu.CompilerParams(
-            collective_id=0, has_side_effects=True, vmem_limit_bytes=40 * 1024 * 1024
+            collective_id=0, has_side_effects=True
         ),
     )(block_order, first_block, block_fill, queries, key_rows, value_rows, grad_out, rab_table)
 

time: 38.9 us -> 34.2 us (0.88)
  local copies, waits for them, and re-layouts: 9.12 us -> 4.04 us
  Pallas kernels: 28.8 us -> 29.3 us
    unnamed x20 -> x10, local copies, waits for them, and re-layouts: 9.12 us -> 4.04 us
    pallas_call x1, Pallas kernels: 28.8 us -> 29.3 us  [four_block_device(): pl.pallas_call(functools.partial(fused_kernel, n_dp, heads, bucket_total)...]
where the time goes in v2:
time: 34.2 us; the launch traced here: 34 us
  Pallas kernels  29.3 us (86%)
  local copies, waits for them, and re-layouts  4.04 us (12%)
  between operations  0.65 us (2%)
    pallas_call x1, Pallas kernels, four_block_device(): pl.pallas_call(functools.partial(fused_kernel, n_dp, heads, bucket_total)...  29.3 us
    unnamed x10, local copies, waits for them, and re-layouts  4.04 us

profile of v2, /device:TPU:0, one launch (start us, length us, event | category | flops | bytes accessed | tf_op | source)
XLA Modules:
  0.0 34.0 jit_solution(7243475440184682840)
XLA Ops:
  0.6 29.3 %shard_map.111 = (bf16[256,512]{1,0:T(8,128)(2,1)}, bf16[256,512]{1,0:T(8,128)(2,1)}, bf16[256,512]{1,0:T(8,128)(2,1)}, f32[4,13]{1,0:T(4,128)}) custom-call(s32[1,4]{1,0:T(1,128)} %order_hbm.1, s32[1,4]{1,0:T(1,128)} %first_hbm.1, s32[1,4]{1,0:T(1,128)} %fill_hbm.1, bf16[256,512]{1,0:T(8,128)(2,1)} %q_hbm.1, bf16[256,512]{1,0:T(8,128)(2,1)} %k_hbm.1, ...), custom_call_target="tpu_custom_call" | custom-call | tf_op jit(solution)/shard_map/pallas_call | solution.py:356
  30.0 0.0 copy-start.1
  30.0 1.7 %copy.16 = bf16[256,512]{1,0:T(8,128)(2,1)} copy(bf16[256,512]{1,0:T(8,128)(2,1)} %get-tuple-element.8) | data formatting | bytes 524288
  31.7 0.0 copy-done.1
  31.7 0.0 copy-start
  31.7 0.7 %copy.17 = bf16[256,512]{1,0:T(8,128)(2,1)} copy(bf16[256,512]{1,0:T(8,128)(2,1)S(1)} %copy-done.1) | data formatting | bytes 524288
  32.4 0.3 copy-done
  32.7 0.0 copy-start.2
  32.7 0.7 %copy.18 = bf16[256,512]{1,0:T(8,128)(2,1)} copy(bf16[256,512]{1,0:T(8,128)(2,1)S(1)} %copy-done) | data formatting | bytes 524288
  33.4 0.0 copy-done.2
  33.4 0.6 %copy.19 = f32[4,13]{1,0:T(4,128)} copy(f32[4,13]{1,0:T(4,128)S(1)} %copy-done.2) | data formatting | bytes 416
Async XLA Ops:
  30.0 1.7 %copy-start.1 = (bf16[256,512]{1,0:T(8,128)(2,1)S(1)}, bf16[256,512]{1,0:T(8,128)(2,1)}, u32[]{:S(2)}) copy-start(bf16[256,512]{1,0:T(8,128)(2,1)} %get-tuple-element.9) | copy-start | bytes 786436
  31.7 1.0 %copy-start = (bf16[256,512]{1,0:T(8,128)(2,1)S(1)}, bf16[256,512]{1,0:T(8,128)(2,1)}, u32[]{:S(2)}) copy-start(bf16[256,512]{1,0:T(8,128)(2,1)} %get-tuple-element.10) | copy-start | bytes 786436
  32.7 0.7 %copy-start.2 = (f32[4,13]{1,0:T(4,128)S(1)}, f32[4,13]{1,0:T(4,128)}, u32[]{:S(2)}) copy-start(f32[4,13]{1,0:T(4,128)} %get-tuple-element.11) | copy-start | bytes 628

commit v3 on v2

--- a/solution.py
+++ b/solution.py
@@ -81,6 +81,22 @@
     rd_send,
     rd_recv,
 ):
+    rows = q_ref.shape[0]
+    dim = q_ref.shape[1] // head_count
+    scale = dim ** (-0.5)
+    blocks = 4
+    dp = lax.axis_index("dp")
+    me = lax.axis_index("ctx")
+    sib = me + 1 - 2 * (me % 2)
+    cross = (me + 2) % 4
+    diag = (sib + 2) % 4
+
+    barrier = pltpu.get_barrier_semaphore()
+    for step in range(1, blocks):
+        pl.semaphore_signal(barrier, inc=1, device_id=(dp, (me + step) % blocks), device_id_type=MESH)
+    for step in range(1, n_dp):
+        pl.semaphore_signal(barrier, inc=1, device_id=((dp + step) % n_dp, me), device_id_type=MESH)
+
     fetches = [
         pltpu.make_async_copy(source, target, in_sems.at[index])
         for index, (source, target) in enumerate((
@@ -90,21 +106,6 @@
     ]
     for fetch in fetches:
         fetch.start()
-    rows = q_ref.shape[0]
-    dim = q_ref.shape[1] // head_count
-    scale = dim ** (-0.5)
-    blocks = 4
-    dp = lax.axis_index("dp")
-    me = lax.axis_index("ctx")
-    sib = me + 1 - 2 * (me % 2)
-    cross = (me + 2) % 4
-    diag = (sib + 2) % 4
-
-    barrier = pltpu.get_barrier_semaphore()
-    for step in range(1, blocks):
-        pl.semaphore_signal(barrier, inc=1, device_id=(dp, (me + step) % blocks), device_id_type=MESH)
-    for step in range(1, n_dp):
-        pl.semaphore_signal(barrier, inc=1, device_id=((dp + step) % n_dp, me), device_id_type=MESH)
 
     for fetch in fetches:
         fetch.wait()
@@ -342,6 +343,19 @@
     rab_ref[...] = total[:head_count, :bucket_total]
 
 
+def hand_over(*refs):
+    sources, targets, held, in_sems, out_sems = refs[:4], refs[4:8], refs[8:12], refs[12], refs[13]
+    loads = [pltpu.make_async_copy(sources[i], held[i], in_sems.at[i]) for i in range(4)]
+    stores = [pltpu.make_async_copy(held[i], targets[i], out_sems.at[i]) for i in range(4)]
+    for load in loads:
+        load.start()
+    for load, store in zip(loads, stores):
+        load.wait()
+        store.start()
+    for store in stores:
+        store.wait()
+
+
 def four_block_device(
     n_dp, queries, key_rows, value_rows, grad_out, rab_table, first_block, block_fill, block_order
 ):
@@ -353,7 +367,7 @@
     buf = pltpu.VMEM((heads, 2, rows, dim), BF16)
     acc = pltpu.VMEM((heads, rows, dim), F32)
     dma = pltpu.SemaphoreType.DMA
-    return pl.pallas_call(
+    outs = pl.pallas_call(
         functools.partial(fused_kernel, n_dp, heads, bucket_total),
         out_shape=(out, out, out, jax.ShapeDtypeStruct((heads, bucket_total), F32)),
         in_specs=[pl.BlockSpec(memory_space=pltpu.HBM)] * 8,
@@ -381,6 +395,14 @@
             collective_id=0, has_side_effects=True
         ),
     )(block_order, first_block, block_fill, queries, key_rows, value_rows, grad_out, rab_table)
+    hbm = pl.BlockSpec(memory_space=pltpu.HBM)
+    return pl.pallas_call(
+        hand_over,
+        out_shape=tuple(jax.ShapeDtypeStruct(one.shape, one.dtype) for one in outs),
+        in_specs=[hbm] * 4,
+        out_specs=(hbm,) * 4,
+        scratch_shapes=[pltpu.VMEM(one.shape, one.dtype) for one in outs] + [dma((4,)), dma((4,))],
+    )(*outs)
 
 
 def bucket_of(distance, bucket_total):

time: 34.2 us -> 32 us (0.936)
  local copies, waits for them, and re-layouts: 4.04 us -> 0 us
  Pallas kernels: 29.3 us -> 31.2 us
    unnamed x10 -> x0, local copies, waits for them, and re-layouts: 4.04 us -> none
    pallas_call x0 -> x1, Pallas kernels: none -> 1.9 us  [four_block_device(): pl.pallas_call(hand_over, out_shape=tuple((jax.ShapeDtypeStruct(one.shape...]
where the time goes in v3:
time: 32 us; the launch traced here: 31.8 us
  Pallas kernels  31.2 us (98%)
  between operations  0.64 us (2%)
    pallas_call x1, Pallas kernels, four_block_device(): pl.pallas_call(functools.partial(fused_kernel, n_dp, heads, bucket_total)...  29.3 us
    pallas_call x1, Pallas kernels, four_block_device(): pl.pallas_call(hand_over, out_shape=tuple((jax.ShapeDtypeStruct(one.shape...  1.9 us

profile of v3, /device:TPU:0, one launch (start us, length us, event | category | flops | bytes accessed | tf_op | source)
XLA Modules:
  0.0 31.8 jit_solution(13287917958388776040)
XLA Ops:
  0.6 29.3 %shard_map.111 = (bf16[256,512]{1,0:T(8,128)(2,1)}, bf16[256,512]{1,0:T(8,128)(2,1)}, bf16[256,512]{1,0:T(8,128)(2,1)}, f32[4,13]{1,0:T(4,128)}) custom-call(s32[1,4]{1,0:T(1,128)} %order_hbm.1, s32[1,4]{1,0:T(1,128)} %first_hbm.1, s32[1,4]{1,0:T(1,128)} %fill_hbm.1, bf16[256,512]{1,0:T(8,128)(2,1)} %q_hbm.1, bf16[256,512]{1,0:T(8,128)(2,1)} %k_hbm.1, ...), custom_call_target="tpu_custom_call" | custom-call | tf_op jit(solution)/shard_map/pallas_call | solution.py:370
  29.9 1.9 %shard_map.112 = (bf16[256,512]{1,0:T(8,128)(2,1)}, bf16[256,512]{1,0:T(8,128)(2,1)}, bf16[256,512]{1,0:T(8,128)(2,1)}, f32[4,13]{1,0:T(4,128)}) custom-call(bf16[256,512]{1,0:T(8,128)(2,1)} %get-tuple-element.8.refs_0_, bf16[256,512]{1,0:T(8,128)(2,1)} %get-tuple-element.9.refs_1_, bf16[256,512]{1,0:T(8,128)(2,1)} %get-tuple-element.10.refs_2_, ...), custom_call_target="tpu_custom_call" | custom-call | tf_op jit(solution)/shard_map/pallas_call | solution.py:399

commit v4 on v3

--- a/solution.py
+++ b/solution.py
@@ -68,6 +68,7 @@
     accv,
     biasv,
     rabs,
+    rab_rows,
     ctx_slots,
     dp_slots,
     s1_send,
@@ -267,6 +268,17 @@
 
     lax.fori_loop(0, head_count, own_step, 0)
 
+    lane_sum = lax.broadcasted_iota(jnp.int32, (8, 2 * rows), 1)
+    offset_sum = lax.broadcasted_iota(jnp.int32, (8, 2 * rows), 0) - jnp.where(
+        lane_sum < rows, lane_sum, lane_sum - 2 * rows
+    )
+    sum_buckets = (
+        bucket_count(jnp.maximum(offset_sum, 0), bucket_total),
+        bucket_count(jnp.abs(delta_a * rows + offset_sum), bucket_total),
+        bucket_count(jnp.abs(delta_b * rows + offset_sum), bucket_total),
+    )
+    lane_out = lax.broadcasted_iota(jnp.int32, (1, 128), 1)
+
     def other_step(h, carry):
         at = cols(h)
         copy2(h).wait_recv()
@@ -280,31 +292,19 @@
         gq_ref[:, at] = ((accq[h] + q_a + q_b) * scale).astype(BF16)
         gk_ref[:, at] = ((acck[h] + k_a + k_b) * scale).astype(BF16)
         gv_ref[:, at] = jnp.where(ok, accv[h] + v_a + v_b, 0.0).astype(BF16)
-        return carry
-
-    lax.fori_loop(0, head_count, other_step, 0)
-
-    lane_out = lax.broadcasted_iota(jnp.int32, (head_count, 128), 1)
-    lane_sum = lax.broadcasted_iota(jnp.int32, (8, 2 * rows), 1)
-    offset_sum = lax.broadcasted_iota(jnp.int32, (8, 2 * rows), 0) - jnp.where(
-        lane_sum < rows, lane_sum, lane_sum - 2 * rows
-    )
-    sum_buckets = (
-        bucket_count(jnp.maximum(offset_sum, 0), bucket_total),
-        bucket_count(jnp.abs(delta_a * rows + offset_sum), bucket_total),
-        bucket_count(jnp.abs(delta_b * rows + offset_sum), bucket_total),
-    )
-    mine = jnp.zeros((head_count, 128), F32)
-    for b in range(bucket_total):
-        here = [sum_buckets[kind] == b for kind in range(3)]
-        per_head = []
-        for h in range(head_count):
+        row = jnp.zeros((1, 128), F32)
+        for b in range(bucket_total):
             picked = jnp.zeros((8, 2 * rows), F32)
             for kind in range(3):
-                picked = picked + jnp.where(here[kind], rabs[kind, h], 0.0)
-            per_head.append(jnp.sum(picked, axis=0, keepdims=True))
-        sums = jnp.sum(jnp.concatenate(per_head, axis=0), axis=1, keepdims=True)
-        mine = jnp.where(lane_out == b, sums, mine)
+                picked = picked + jnp.where(sum_buckets[kind] == b, rabs[kind, h], 0.0)
+            folded = jnp.sum(picked, axis=0, keepdims=True)
+            row = jnp.where(lane_out == b, jnp.sum(folded, axis=1, keepdims=True), row)
+        rab_rows[h] = row
+        return carry
+
+    lax.fori_loop(0, head_count, other_step, 0)
+
+    mine = jnp.concatenate([rab_rows[h] for h in range(head_count)], axis=0)
     ctx_slots[me] = jnp.concatenate([mine, jnp.zeros((8 - head_count, 128), F32)], axis=0)
 
     def rab_ctx(step, owner):
@@ -386,6 +386,7 @@
             acc, acc, acc,
             pltpu.VMEM((3, heads, 1, 2 * rows), F32),
             pltpu.VMEM((3, heads, 8, 2 * rows), F32),
+            pltpu.VMEM((heads, 1, 128), F32),
             pltpu.VMEM((4, 8, 128), F32),
             pltpu.VMEM((n_dp, 8, 128), F32),
             dma((heads,)), dma((heads,)), dma((heads,)), dma((heads,)), dma((heads,)), dma((heads,)),

time: 32 us -> 31.7 us (level)
  no operation moved by 1% of the time
where the time goes in v4:
time: 31.7 us; the launch traced here: 31.5 us
  Pallas kernels  30.9 us (97%)
  between operations  0.64 us (2%)
    pallas_call x1, Pallas kernels, four_block_device(): pl.pallas_call(functools.partial(fused_kernel, n_dp, heads, bucket_total)...  29 us
    pallas_call x1, Pallas kernels, four_block_device(): pl.pallas_call(hand_over, out_shape=tuple((jax.ShapeDtypeStruct(one.shape...  1.9 us

profile of v4, /device:TPU:0, one launch (start us, length us, event | category | flops | bytes accessed | tf_op | source)
XLA Modules:
  0.0 31.5 jit_solution(10679542476444899803)
XLA Ops:
  0.6 29.0 %shard_map.111 = (bf16[256,512]{1,0:T(8,128)(2,1)}, bf16[256,512]{1,0:T(8,128)(2,1)}, bf16[256,512]{1,0:T(8,128)(2,1)}, f32[4,13]{1,0:T(4,128)}) custom-call(s32[1,4]{1,0:T(1,128)} %order_hbm.1, s32[1,4]{1,0:T(1,128)} %first_hbm.1, s32[1,4]{1,0:T(1,128)} %fill_hbm.1, bf16[256,512]{1,0:T(8,128)(2,1)} %q_hbm.1, bf16[256,512]{1,0:T(8,128)(2,1)} %k_hbm.1, ...), custom_call_target="tpu_custom_call" | custom-call | tf_op jit(solution)/shard_map/pallas_call | solution.py:370
  29.6 1.9 %shard_map.112 = (bf16[256,512]{1,0:T(8,128)(2,1)}, bf16[256,512]{1,0:T(8,128)(2,1)}, bf16[256,512]{1,0:T(8,128)(2,1)}, f32[4,13]{1,0:T(4,128)}) custom-call(bf16[256,512]{1,0:T(8,128)(2,1)} %get-tuple-element.8.refs_0_, bf16[256,512]{1,0:T(8,128)(2,1)} %get-tuple-element.9.refs_1_, bf16[256,512]{1,0:T(8,128)(2,1)} %get-tuple-element.10.refs_2_, ...), custom_call_target="tpu_custom_call" | custom-call | tf_op jit(solution)/shard_map/pallas_call | solution.py:400
